TPU v7x, 512 devices: a whole 4x8x8 slice. The times are simulated.
512 devices in a mesh: ctx: 128 (over y, z, core), tp: 4 (over x).
Axes of the slice: x: 4, y: 8, z: 8, core: 2. Of those that a mesh axis runs over, the one named last changes fastest.
Arguments:
- query_rows: bfloat16 [16384, 4096], P('ctx', 'tp'), may hold values from -1.796875 to 1.796875
- key_rows: bfloat16 [16384, 4096], P('ctx', 'tp'), may hold values from -1.796875 to 1.796875
- value_rows: bfloat16 [16384, 4096], P('ctx', 'tp'), may hold values from -6 to 6
- out_grad: bfloat16 [16384, 4096], P('ctx', 'tp'), may hold values from -6 to 6
- slopes: float32 [32], P('tp'), may hold values from 5e-05 to 0.03
- norm_gain: float32 [4096], P('tp'), may hold values from 0.25 to 1.75
- doc_lengths: int32 [16], replicated, may hold values from 1 to 16, 128 in all
Outputs:
- attended: bfloat16 [16384, 4096], P('ctx', 'tp')
- query_gradient: bfloat16 [16384, 4096], P('ctx', 'tp')
- key_gradient: bfloat16 [16384, 4096], P('ctx', 'tp')
- value_gradient: bfloat16 [16384, 4096], P('ctx', 'tp')
Inputs may be any that keep to these rules, and one draw needn't show every extreme that they name: `doc_lengths`: the lengths sum to 128; the longest is exactly 16.
All inputs are finite; a program needn't handle non-finite values.
Results may differ from a plain program's by a relative error of at most 0.013.
Values may be sent and summed in bfloat16 or wider, within the bound.
A program may use at most 192 MiB of HBM per device.

v0:
```python
import functools

import jax
import jax.numpy as jnp
from jax import lax
from jax.experimental import pallas as pl
from jax.experimental.pallas import tpu as pltpu
from jax.sharding import PartitionSpec as P

HD = 128
EPSILON = 1e-06
MESH = pl.DeviceIdType.MESH
F32 = jnp.float32
BF16 = jnp.bfloat16
HEADS = 8
HALF = 4
ZN = 8
SHARE = HALF * HD // ZN
XN = 4


def dot(a, b, ca, cb):
    return lax.dot_general(a, b, (((ca,), (cb,)), ((), ())), preferred_element_type=F32)


def kernel(
    features,
    slopes,
    doc_lengths,
    q_hbm,
    k_hbm,
    v_hbm,
    og_hbm,
    gain,
    att_hbm,
    dq_hbm,
    dk_hbm,
    dv_hbm,
    q,
    k,
    v,
    og,
    att,
    dq,
    dk,
    dv,
    weights,
    raw,
    local,
    sib_out,
    sib_in,
    share_out,
    share_in,
    carry_out,
    carry_in,
    back_out,
    back_in,
    half_out,
    state,
    sums,
    local_sem,
    out_sem,
    sib_send,
    sib_recv,
    share_send,
    share_recv,
    carry_send,
    carry_recv,
    back_send,
    back_recv,
    sums_send,
    sums_recv,
):
    ctx = lax.axis_index("ctx")
    x = lax.axis_index("tp")
    rows_y = lax.axis_size("ctx") // (2 * ZN)
    core = lax.rem(ctx, 2)
    z = lax.rem(ctx // 2, ZN)
    y = ctx // (2 * ZN)
    is0 = core == 0
    sib = (y * (2 * ZN) + z * 2 + (1 - core), x)

    def at_z(other):
        return (y * (2 * ZN) + other * 2 + core, x)

    up = (lax.rem(y + 1, rows_y) * (2 * ZN) + z * 2 + core, x)
    down = (lax.rem(y + rows_y - 1, rows_y) * (2 * ZN) + z * 2 + core, x)
    offsets = (4, 3, 5, 2, 6, 1, 7)
    ring = [lax.rem(z + d, ZN) for d in offsets]
    cross = [lax.rem(x + d, XN) for d in (2, 1, 3)]

    barrier = pltpu.get_barrier_semaphore()
    for other in ring:
        pl.semaphore_signal(barrier, 1, device_id=at_z(other), device_id_type=MESH)
    for other in cross:
        pl.semaphore_signal(barrier, 1, device_id=(ctx, other), device_id_type=MESH)
    for other in (up, down, sib):
        pl.semaphore_signal(barrier, 1, device_id=other, device_id_type=MESH)

    loads = [
        pltpu.make_async_copy(src, dst, local_sem.at[i])
        for i, (src, dst) in enumerate(((k_hbm, k), (v_hbm, v), (q_hbm, q), (og_hbm, og)))
    ]
    for load in loads:
        load.start()

    starts = [jnp.int32(0)]
    for j in range(doc_lengths.shape[0] - 1):
        starts.append(starts[-1] + doc_lengths[j])

    def carries(block):
        hit = starts[0] == block
        for start in starts[1:]:
            hit = hit | (start == block)
        return jnp.where(hit, F32(0.0), F32(1.0))

    row_first = y * (2 * ZN)
    flags = [carries(row_first + i) for i in range(2 * ZN)]
    flag0 = carries(row_first + 2 * z)
    flag1 = carries(row_first + 2 * z + 1)
    flag = jnp.where(is0, flag0, flag1)
    share_head = HALF * core + z // (ZN // HALF)
    lam_share = jnp.exp(jnp.full((1, HD), -HD * 1.0, F32) * slopes[share_head])
    lam2 = lam_share * lam_share
    step_decay = [lam2 * (flags[2 * j] * flags[2 * j + 1]) for j in range(ZN)]

    token = lax.broadcasted_iota(jnp.int32, (HD, HD), 0).astype(F32)
    column = lax.broadcasted_iota(jnp.int32, (HD, HD), 1).astype(F32)
    distance = token - column

    def within(h):
        return jnp.where(distance >= 0.0, jnp.exp(-slopes[h] * jnp.maximum(distance, 0.0)), 0.0)

    def entry(h):
        return jnp.exp(-slopes[h] * (token + 1.0)) * flag

    def tail(h):
        return jnp.exp(-slopes[h] * (HD - 1.0 - token))

    def lam_of(h):
        return jnp.exp(jnp.full((1, HD), -HD * 1.0, F32) * slopes[h])

    def cols(h):
        return pl.ds(h * HD, HD)

    mine = HALF * core
    theirs = HALF * (1 - core)

    def remote(src, dst, send, recv, device):
        return pltpu.make_async_remote_copy(
            src_ref=src,
            dst_ref=dst,
            send_sem=send,
            recv_sem=recv,
            device_id=device,
            device_id_type=MESH,
        )

    def scan(phase, backward):
        sends = []
        for other in ring:
            copy = remote(
                share_out.at[phase, other],
                share_in.at[phase, z],
                share_send.at[phase, other],
                share_recv.at[phase, z],
                at_z(other),
            )
            copy.start()
            sends.append(copy)
        share_in[phase, z] = share_out[phase, z]

        yield

        for other in ring[::-1]:
            remote(
                share_out.at[phase, z],
                share_in.at[phase, other],
                share_send.at[phase, other],
                share_recv.at[phase, other],
                at_z(other),
            ).wait_recv()
        order = range(ZN - 1, -1, -1) if backward else range(ZN)
        total = jnp.zeros((SHARE, HD), F32)
        product = jnp.ones((1, HD), F32)
        before, products = {}, {}
        for j in order:
            before[j], products[j] = total, product
            total = total * step_decay[j] + share_in[phase, j].astype(F32)
            product = product * step_decay[j]
        carry_out[phase] = total.astype(BF16)
        carry = remote(
            carry_out.at[phase],
            carry_in.at[phase],
            carry_send.at[phase],
            carry_recv.at[phase],
            down if backward else up,
        )
        carry.start()
        carry.wait_recv()
        incoming = carry_in[phase].astype(F32)
        for j in range(ZN):
            back_out[phase, j] = (before[j] + products[j] * incoming).astype(BF16)
        for other in ring:
            copy = remote(
                back_out.at[phase, other],
                back_in.at[phase, z],
                back_send.at[phase, other],
                back_recv.at[phase, z],
                at_z(other),
            )
            copy.start()
            sends.append(copy)
        back_in[phase, z] = back_out[phase, z]

        yield

        for other in ring[::-1]:
            remote(
                back_out.at[phase, z],
                back_in.at[phase, other],
                back_send.at[phase, other],
                back_recv.at[phase, other],
                at_z(other),
            ).wait_recv()
        for copy in sends:
            copy.wait_send()
        carry.wait_send()
        yield

    def head_of(buffer, phase, i):
        per = ZN // HALF
        return jnp.concatenate([buffer[phase, per * i + j] for j in range(per)], axis=0)

    def put_head(buffer, phase, i, value):
        per = ZN // HALF
        for j in range(per):
            buffer[phase, per * i + j] = value[j * SHARE : (j + 1) * SHARE]

    loads[0].wait()
    loads[1].wait()
    for h in range(HEADS):
        value_decayed = (tail(h) * v[:, cols(h)].astype(F32)).astype(BF16)
        local[h] = dot(k[:, cols(h)], value_decayed, 0, 0)
    for i in range(HALF):
        sib_out[0, i] = local[theirs + i].astype(BF16)

    pl.semaphore_wait(barrier, len(ring) + len(cross) + 3)

    sib_copy = remote(sib_out.at[0], sib_in.at[0], sib_send.at[0], sib_recv.at[0], sib)
    sib_copy.start()
    sib_copy.wait_recv()
    for i in range(HALF):
        lam = lam_of(mine + i)
        own, other = local[mine + i], sib_in[0, i].astype(F32)
        first, second = jnp.where(is0, own, other), jnp.where(is0, other, own)
        put_head(share_out, 0, i, (first * (lam * flag1) + second).astype(BF16))
    forward = scan(0, False)
    next(forward)

    loads[2].wait()
    loads[3].wait()
    for h in range(HEADS):
        scores = dot(q[:, cols(h)], k[:, cols(h)], 1, 1)
        weight = (scores * within(h)).astype(BF16)
        weights[h] = weight
        raw[:, cols(h)] = dot(weight, v[:, cols(h)], 1, 0)

    next(forward)
    next(forward)
    for i in range(HALF):
        lam = lam_of(mine + i)
        own, other = local[mine + i], sib_in[0, i].astype(F32)
        first = jnp.where(is0, own, other)
        arrived = head_of(back_in, 0, i).astype(F32)
        later = arrived * (lam * flag0) + first
        state[0, mine + i] = jnp.where(is0, arrived, later).astype(BF16)
        half_out[0, i] = jnp.where(is0, later, arrived).astype(BF16)
    half_copy = remote(
        half_out.at[0], state.at[0, pl.ds(mine, HALF)], sib_send.at[1], sib_recv.at[1], sib
    )
    half_copy.start()
    half_copy.wait_recv()

    squares = jnp.zeros((HD, HD), F32)
    products = jnp.zeros((HD, HD), F32)
    for h in range(HEADS):
        raw_h = raw[:, cols(h)] + dot(q[:, cols(h)], state[0, h], 1, 0) * entry(h)
        raw[:, cols(h)] = raw_h
        squares = squares + raw_h * raw_h
        products = products + raw_h * (og[:, cols(h)].astype(F32) * gain[:, cols(h)])
    square_row = jnp.sum(squares.T, axis=0, keepdims=True)
    product_row = jnp.sum(products.T, axis=0, keepdims=True)
    upper = lax.broadcasted_iota(jnp.int32, (8, HD), 0) < 4
    sums[x] = jnp.where(upper, square_row, product_row)
    sum_copies = []
    for other in cross:
        copy = remote(
            sums.at[x], sums.at[x], sums_send.at[other], sums_recv.at[x], (ctx, other)
        )
        copy.start()
        sum_copies.append(copy)
    for other in cross[::-1]:
        remote(
            sums.at[x], sums.at[other], sums_send.at[other], sums_recv.at[other], (ctx, other)
        ).wait_recv()
    total = sums[0] + sums[1] + sums[2] + sums[3]
    inverse_row = lax.rsqrt(total[0:1] / features + EPSILON)
    factor_row = inverse_row * inverse_row * inverse_row * total[4:5] / features
    inverse = jnp.broadcast_to(inverse_row, (HD, HD)).T
    factor = jnp.broadcast_to(factor_row, (HD, HD)).T

    for h in range(HEADS):
        scaled = og[:, cols(h)].astype(F32) * gain[:, cols(h)]
        grad = (inverse * scaled - factor * raw[:, cols(h)]).astype(BF16)
        og[:, cols(h)] = grad
        query_decayed = (entry(h) * q[:, cols(h)].astype(F32)).astype(BF16)
        local[h] = dot(query_decayed, grad, 0, 0)
    for i in range(HALF):
        sib_out[1, i] = local[theirs + i].astype(BF16)
    sib_copy2 = remote(sib_out.at[1], sib_in.at[1], sib_send.at[2], sib_recv.at[2], sib)
    sib_copy2.start()
    sib_copy2.wait_recv()
    for i in range(HALF):
        lam = lam_of(mine + i)
        own, other = local[mine + i], sib_in[1, i].astype(F32)
        first, second = jnp.where(is0, own, other), jnp.where(is0, other, own)
        put_head(share_out, 1, i, (first + second * (lam * flag0)).astype(BF16))
    backward = scan(1, True)
    next(backward)

    stores = []

    def store(src, dst):
        copy = pltpu.make_async_copy(src, dst, out_sem.at[len(stores)])
        copy.start()
        stores.append(copy)

    for h in range(HEADS):
        att[:, cols(h)] = (raw[:, cols(h)] * inverse * gain[:, cols(h)]).astype(BF16)
    store(att, att_hbm)
    for h in range(HEADS):
        grad = og[:, cols(h)]
        dscore = (dot(grad, v[:, cols(h)], 1, 1) * within(h)).astype(BF16)
        dq[:, cols(h)] = (
            dot(dscore, k[:, cols(h)], 1, 0) + dot(grad, state[0, h], 1, 1) * entry(h)
        ).astype(BF16)
        dk[:, cols(h)] = dot(dscore, q[:, cols(h)], 0, 0)
        dv[:, cols(h)] = dot(weights[h], grad, 0, 0)
    store(dq, dq_hbm)

    next(backward)
    next(backward)
    for i in range(HALF):
        lam = lam_of(mine + i)
        own, other = local[mine + i], sib_in[1, i].astype(F32)
        second = jnp.where(is0, other, own)
        arrived = head_of(back_in, 1, i).astype(F32)
        earlier = arrived * (lam * flag1) + second
        state[1, mine + i] = jnp.where(is0, earlier, arrived).astype(BF16)
        half_out[1, i] = jnp.where(is0, arrived, earlier).astype(BF16)
    half_copy2 = remote(
        half_out.at[1], state.at[1, pl.ds(mine, HALF)], sib_send.at[3], sib_recv.at[3], sib
    )
    half_copy2.start()
    half_copy2.wait_recv()

    stores[0].wait()
    stores[1].wait()
    for h in range(HEADS):
        grad_state = state[1, h]
        att[:, cols(h)] = (
            dk[:, cols(h)] + dot(v[:, cols(h)], grad_state, 1, 1) * tail(h)
        ).astype(BF16)
    store(att, dk_hbm)
    for h in range(HEADS):
        grad_state = state[1, h]
        dq[:, cols(h)] = (
            dv[:, cols(h)] + dot(k[:, cols(h)], grad_state, 1, 0) * tail(h)
        ).astype(BF16)
    store(dq, dv_hbm)

    sib_copy.wait_send()
    half_copy.wait_send()
    sib_copy2.wait_send()
    half_copy2.wait_send()
    for copy in sum_copies:
        copy.wait_send()
    stores[2].wait()
    stores[3].wait()


def body(query_rows, key_rows, value_rows, out_grad, slopes, norm_gain, doc_lengths):
    rows, width = query_rows.shape
    features = width * lax.axis_size("tp")
    whole = jax.ShapeDtypeStruct((rows, width), BF16)
    smem = pl.BlockSpec(memory_space=pltpu.SMEM)
    anywhere = pl.BlockSpec(memory_space=pl.ANY)
    dma = pltpu.SemaphoreType.DMA
    return pl.pallas_call(
        functools.partial(kernel, features),
        out_shape=(whole,) * 4,
        in_specs=[smem, smem]
        + [anywhere] * 4
        + [pl.BlockSpec(memory_space=pltpu.VMEM)],
        out_specs=(anywhere,) * 4,
        scratch_shapes=[
            pltpu.VMEM((rows, width), BF16),
            pltpu.VMEM((rows, width), BF16),
            pltpu.VMEM((rows, width), BF16),
            pltpu.VMEM((rows, width), BF16),
            pltpu.VMEM((rows, width), BF16),
            pltpu.VMEM((rows, width), BF16),
            pltpu.VMEM((rows, width), F32),
            pltpu.VMEM((rows, width), F32),
            pltpu.VMEM((HEADS, HD, HD), BF16),
            pltpu.VMEM((rows, width), F32),
            pltpu.VMEM((HEADS, HD, HD), F32),
            pltpu.VMEM((2, HALF, HD, HD), BF16),
            pltpu.VMEM((2, HALF, HD, HD), BF16),
            pltpu.VMEM((2, ZN, SHARE, HD), BF16),
            pltpu.VMEM((2, ZN, SHARE, HD), BF16),
            pltpu.VMEM((2, SHARE, HD), BF16),
            pltpu.VMEM((2, SHARE, HD), BF16),
            pltpu.VMEM((2, ZN, SHARE, HD), BF16),
            pltpu.VMEM((2, ZN, SHARE, HD), BF16),
            pltpu.VMEM((2, HALF, HD, HD), BF16),
            pltpu.VMEM((2, HEADS, HD, HD), BF16),
            pltpu.VMEM((XN, 8, HD), F32),
            dma((4,)),
            dma((4,)),
            dma((4,)),
            dma((4,)),
            dma((2, ZN)),
            dma((2, ZN)),
            dma((2,)),
            dma((2,)),
            dma((2, ZN)),
            dma((2, ZN)),
            dma((XN,)),
            dma((XN,)),
        ],
        compiler_params=pltpu.CompilerParams(
            collective_id=0, has_side_effects=True, vmem_limit_bytes=32 * 1024 * 1024
        ),
        name="lightning",
    )(
        slopes,
        doc_lengths,
        query_rows,
        key_rows,
        value_rows,
        out_grad,
        norm_gain.reshape(1, width),
    )


def solution(mesh):
    spec = P("ctx", "tp")
    in_specs = (spec, spec, spec, spec, P("tp"), P("tp"), P())
    return jax.shard_map(
        body, mesh=mesh, in_specs=in_specs, out_specs=(spec,) * 4, check_vma=False
    )
```

profile of v0, /device:TPU:1, one launch (start us, length us, event | category | flops | bytes accessed | tf_op | source)
XLA Modules:
  0.0 58.9 jit_solution(12093966576707394798)
XLA Ops:
  0.6 0.0 copy-start.6
  0.6 0.0 copy-start.5
  0.7 0.6 %copy-done.6 = s32[16]{0:T(128)S(1)} copy-done((s32[16]{0:T(128)S(1)}, s32[16]{0:T(128)}, u32[]{:S(2)}) %copy-start.6) | copy-done | bytes 88
  1.3 0.0 copy-done.5
  1.3 0.0 copy-start
  1.3 0.9 %copy-done = bf16[128,1024]{1,0:T(8,128)(2,1)S(1)} copy-done((bf16[128,1024]{1,0:T(8,128)(2,1)S(1)}, bf16[128,1024]{1,0:T(8,128)(2,1)}, u32[]{:S(2)}) %copy-start) | copy-done | bytes 262168
  2.3 0.0 copy-start.1
  2.3 0.9 %copy-done.1 = bf16[128,1024]{1,0:T(8,128)(2,1)S(1)} copy-done((bf16[128,1024]{1,0:T(8,128)(2,1)S(1)}, bf16[128,1024]{1,0:T(8,128)(2,1)}, u32[]{:S(2)}) %copy-start.1) | copy-done | bytes 262168
  3.2 0.0 copy-start.2
  3.2 0.9 %copy-done.2 = bf16[128,1024]{1,0:T(8,128)(2,1)S(1)} copy-done((bf16[128,1024]{1,0:T(8,128)(2,1)S(1)}, bf16[128,1024]{1,0:T(8,128)(2,1)}, u32[]{:S(2)}) %copy-start.2) | copy-done | bytes 262168
  4.2 0.0 copy-start.3
  4.2 0.9 %copy-done.3 = bf16[128,1024]{1,0:T(8,128)(2,1)S(1)} copy-done((bf16[128,1024]{1,0:T(8,128)(2,1)S(1)}, bf16[128,1024]{1,0:T(8,128)(2,1)}, u32[]{:S(2)}) %copy-start.3) | copy-done | bytes 262168
  5.1 0.0 copy-start.4
  5.1 0.7 %copy-done.4 = f32[1024]{0:T(1024)S(1)} copy-done((f32[1024]{0:T(1024)S(1)}, f32[1024]{0:T(1024)}, u32[]{:S(2)}) %copy-start.4) | copy-done | bytes 4120
  5.8 50.3 %lightning.1 = (bf16[128,1024]{1,0:T(8,128)(2,1)S(1)}, bf16[128,1024]{1,0:T(8,128)(2,1)S(1)}, bf16[128,1024]{1,0:T(8,128)(2,1)S(1)}, bf16[128,1024]{1,0:T(8,128)(2,1)S(1)}) custom-call(f32[8]{0:T(128)S(1)} %copy-done.5, s32[16]{0:T(128)S(1)} %copy-done.6, bf16[128,1024]{1,0:T(8,128)(2,1)S(1)} %copy-done, bf16[128,1024]{1,0:T(8,128)(2,1)S(1)} %copy-done.1, ...), custom_call_target="tpu_custom_call" | custom-call | tf_op jit(solution)/shard_map/lightning/pallas_call | solution.py:400
  56.1 0.7 %copy.15 = bf16[128,1024]{1,0:T(8,128)(2,1)} copy(bf16[128,1024]{1,0:T(8,128)(2,1)S(1)} %get-tuple-element.8) | data formatting | bytes 524288
  56.8 0.7 %copy.16 = bf16[128,1024]{1,0:T(8,128)(2,1)} copy(bf16[128,1024]{1,0:T(8,128)(2,1)S(1)} %get-tuple-element.9) | data formatting | bytes 524288
  57.5 0.7 %copy.17 = bf16[128,1024]{1,0:T(8,128)(2,1)} copy(bf16[128,1024]{1,0:T(8,128)(2,1)S(1)} %get-tuple-element.10) | data formatting | bytes 524288
  58.2 0.7 %copy.18 = bf16[128,1024]{1,0:T(8,128)(2,1)} copy(bf16[128,1024]{1,0:T(8,128)(2,1)S(1)} %get-tuple-element.11) | data formatting | bytes 524288
Async XLA Ops:
  0.6 0.7 %copy-start.6 = (s32[16]{0:T(128)S(1)}, s32[16]{0:T(128)}, u32[]{:S(2)}) copy-start(s32[16]{0:T(128)} %doc_lengths.1) | copy-start | bytes 196
  0.6 0.7 %copy-start.5 = (f32[8]{0:T(128)S(1)}, f32[8]{0:T(128)}, u32[]{:S(2)}) copy-start(f32[8]{0:T(128)} %slopes.1) | copy-start | bytes 100
  1.3 0.9 %copy-start = (bf16[128,1024]{1,0:T(8,128)(2,1)S(1)}, bf16[128,1024]{1,0:T(8,128)(2,1)}, u32[]{:S(2)}) copy-start(bf16[128,1024]{1,0:T(8,128)(2,1)} %q_hbm.1) | copy-start | bytes 786436
  2.3 0.9 %copy-start.1 = (bf16[128,1024]{1,0:T(8,128)(2,1)S(1)}, bf16[128,1024]{1,0:T(8,128)(2,1)}, u32[]{:S(2)}) copy-start(bf16[128,1024]{1,0:T(8,128)(2,1)} %k_hbm.1) | copy-start | bytes 786436
  3.2 0.9 %copy-start.2 = (bf16[128,1024]{1,0:T(8,128)(2,1)S(1)}, bf16[128,1024]{1,0:T(8,128)(2,1)}, u32[]{:S(2)}) copy-start(bf16[128,1024]{1,0:T(8,128)(2,1)} %v_hbm.1) | copy-start | bytes 786436
  4.2 0.9 %copy-start.3 = (bf16[128,1024]{1,0:T(8,128)(2,1)S(1)}, bf16[128,1024]{1,0:T(8,128)(2,1)}, u32[]{:S(2)}) copy-start(bf16[128,1024]{1,0:T(8,128)(2,1)} %og_hbm.1) | copy-start | bytes 786436
  5.1 0.7 %copy-start.4 = (f32[1024]{0:T(1024)S(1)}, f32[1024]{0:T(1024)}, u32[]{:S(2)}) copy-start(f32[1024]{0:T(1024)} %param.12) | copy-start | bytes 12292
where the time goes:
time: 59.2 us; the launch traced here: 58.9 us
  Pallas kernels  50.3 us (85%)
  local copies, waits for them, and re-layouts  7.95 us (13%)
  between operations  0.66 us (1%)
    pallas_call x1, Pallas kernels, body(): pl.pallas_call(functools.partial(kernel, features), out_shape=(whole,) *...  50.3 us
    unnamed x18, local copies, waits for them, and re-layouts  7.95 us

commit v1 on v0

--- a/solution.py
+++ b/solution.py
@@ -25,17 +25,21 @@
 
 def kernel(
     features,
-    slopes,
-    doc_lengths,
+    slopes_hbm,
+    doc_hbm,
     q_hbm,
     k_hbm,
     v_hbm,
     og_hbm,
-    gain,
+    gain_hbm,
     att_hbm,
     dq_hbm,
     dk_hbm,
     dv_hbm,
+    slopes,
+    doc_lengths,
+    gain_flat,
+    gain,
     q,
     k,
     v,
@@ -99,10 +103,25 @@
 
     loads = [
         pltpu.make_async_copy(src, dst, local_sem.at[i])
-        for i, (src, dst) in enumerate(((k_hbm, k), (v_hbm, v), (q_hbm, q), (og_hbm, og)))
+        for i, (src, dst) in enumerate(
+            (
+                (k_hbm, k),
+                (v_hbm, v),
+                (q_hbm, q),
+                (og_hbm, og),
+                (slopes_hbm, slopes),
+                (doc_hbm, doc_lengths),
+                (gain_hbm, gain_flat),
+            )
+        )
     ]
     for load in loads:
         load.start()
+
+    for load in loads[4:]:
+        load.wait()
+    for h in range(HEADS):
+        gain[:, h * HD : (h + 1) * HD] = gain_flat[h * HD : (h + 1) * HD].reshape(1, HD)
 
     starts = [jnp.int32(0)]
     for j in range(doc_lengths.shape[0] - 1):
@@ -390,21 +409,34 @@
     stores[3].wait()
 
 
+def place(*refs):
+    sources, targets, sems = refs[:4], refs[4:8], refs[8]
+    copies = [
+        pltpu.make_async_copy(src, dst, sems.at[i])
+        for i, (src, dst) in enumerate(zip(sources, targets))
+    ]
+    for copy in copies:
+        copy.start()
+    for copy in copies:
+        copy.wait()
+
+
 def body(query_rows, key_rows, value_rows, out_grad, slopes, norm_gain, doc_lengths):
     rows, width = query_rows.shape
     features = width * lax.axis_size("tp")
     whole = jax.ShapeDtypeStruct((rows, width), BF16)
-    smem = pl.BlockSpec(memory_space=pltpu.SMEM)
     anywhere = pl.BlockSpec(memory_space=pl.ANY)
     dma = pltpu.SemaphoreType.DMA
-    return pl.pallas_call(
+    results = pl.pallas_call(
         functools.partial(kernel, features),
         out_shape=(whole,) * 4,
-        in_specs=[smem, smem]
-        + [anywhere] * 4
-        + [pl.BlockSpec(memory_space=pltpu.VMEM)],
+        in_specs=[anywhere] * 7,
         out_specs=(anywhere,) * 4,
         scratch_shapes=[
+            pltpu.SMEM(slopes.shape, F32),
+            pltpu.SMEM(doc_lengths.shape, jnp.int32),
+            pltpu.VMEM((width,), F32),
+            pltpu.VMEM((1, width), F32),
             pltpu.VMEM((rows, width), BF16),
             pltpu.VMEM((rows, width), BF16),
             pltpu.VMEM((rows, width), BF16),
@@ -427,7 +459,7 @@
             pltpu.VMEM((2, HALF, HD, HD), BF16),
             pltpu.VMEM((2, HEADS, HD, HD), BF16),
             pltpu.VMEM((XN, 8, HD), F32),
-            dma((4,)),
+            dma((7,)),
             dma((4,)),
             dma((4,)),
             dma((4,)),
@@ -441,7 +473,7 @@
             dma((XN,)),
         ],
         compiler_params=pltpu.CompilerParams(
-            collective_id=0, has_side_effects=True, vmem_limit_bytes=32 * 1024 * 1024
+            collective_id=0, has_side_effects=True, vmem_limit_bytes=60 * 1024 * 1024
         ),
         name="lightning",
     )(
@@ -451,8 +483,17 @@
         key_rows,
         value_rows,
         out_grad,
-        norm_gain.reshape(1, width),
+        norm_gain,
     )
+    return pl.pallas_call(
+        place,
+        out_shape=(whole,) * 4,
+        in_specs=[anywhere] * 4,
+        out_specs=(anywhere,) * 4,
+        scratch_shapes=[dma((4,))],
+        compiler_params=pltpu.CompilerParams(vmem_limit_bytes=60 * 1024 * 1024),
+        name="place",
+    )(*results)
 
 
 def solution(mesh):

time: 59.2 us -> 84.2 us (1.42)
  Pallas kernels: 50.3 us -> 83.4 us
  local copies, waits for them, and re-layouts: 7.95 us -> 0 us
    pallas_call x0 -> x1, Pallas kernels: none -> 32.9 us  [body(): pl.pallas_call(place, out_shape=(whole,) * 4, in_specs=[anywhere] * 4, ou...]
    unnamed x18 -> x0, local copies, waits for them, and re-layouts: 7.95 us -> none
where the time goes in v1:
time: 84.2 us; the launch traced here: 84 us
  Pallas kernels  83.4 us (99%)
    pallas_call x1, Pallas kernels, body(): pl.pallas_call(functools.partial(kernel, features), out_shape=(whole,) *...  50.5 us
    pallas_call x1, Pallas kernels, body(): pl.pallas_call(place, out_shape=(whole,) * 4, in_specs=[anywhere] * 4, ou...  32.9 us

profile of v1, /device:TPU:1, one launch (start us, length us, event | category | flops | bytes accessed | tf_op | source)
XLA Modules:
  0.0 84.0 jit_solution(8736274832685922637)
XLA Ops:
  0.6 50.5 %lightning.1 = (bf16[128,1024]{1,0:T(8,128)(2,1)}, bf16[128,1024]{1,0:T(8,128)(2,1)}, bf16[128,1024]{1,0:T(8,128)(2,1)}, bf16[128,1024]{1,0:T(8,128)(2,1)}) custom-call(f32[8]{0:T(128)} %slopes_hbm.1, s32[16]{0:T(128)} %doc_hbm.1, bf16[128,1024]{1,0:T(8,128)(2,1)} %q_hbm.1, bf16[128,1024]{1,0:T(8,128)(2,1)} %k_hbm.1, bf16[128,1024]{1,0:T(8,128)(2,1)} %v_hbm.1, ...), custom_call_target="tpu_custom_call" | custom-call | tf_op jit(solution)/shard_map/lightning/pallas_call | solution.py:430
  51.1 32.9 %place.1 = (bf16[128,1024]{1,0:T(8,128)(2,1)}, bf16[128,1024]{1,0:T(8,128)(2,1)}, bf16[128,1024]{1,0:T(8,128)(2,1)}, bf16[128,1024]{1,0:T(8,128)(2,1)}) custom-call(bf16[128,1024]{1,0:T(8,128)(2,1)} %get-tuple-element.8.refs_0_, bf16[128,1024]{1,0:T(8,128)(2,1)} %get-tuple-element.9.refs_1_, bf16[128,1024]{1,0:T(8,128)(2,1)} %get-tuple-element.10.refs_2_, ...), custom_call_target="tpu_custom_call" | custom-call | tf_op jit(solution)/shard_map/place/pallas_call | solution.py:488

commit v2 on v1

v2 whole, which is shorter than its diff:
```python
import functools

import jax
import jax.numpy as jnp
from jax import lax
from jax.experimental import pallas as pl
from jax.experimental.pallas import tpu as pltpu
from jax.sharding import PartitionSpec as P

HD = 128
EPSILON = 1e-06
MESH = pl.DeviceIdType.MESH
F32 = jnp.float32
BF16 = jnp.bfloat16
TOK = 128
PAIR = 2 * TOK
HALF = 4
WIDE = HALF * HD
ZN = 8
SHARE = HALF * HD // ZN
PER = ZN // HALF
XN = 4


def dot(a, b, ca, cb):
    return lax.dot_general(a, b, (((ca,), (cb,)), ((), ())), preferred_element_type=F32)


def kernel(
    features,
    slopes_hbm,
    doc_hbm,
    q_hbm,
    k_hbm,
    v_hbm,
    og_hbm,
    gain_hbm,
    att_out,
    dq_out,
    dk_out,
    dv_out,
    slopes,
    doc_lengths,
    gain_flat,
    gain,
    q,
    k,
    v,
    og,
    k_other,
    v_other,
    att,
    dq,
    dk,
    dv,
    table,
    weights,
    raw,
    dk_part,
    dv_part,
    share_out,
    share_in,
    carry_out,
    carry_in,
    back_out,
    back_in,
    sums,
    local_sem,
    own_sem,
    swap_send,
    swap_recv,
    share_send,
    share_recv,
    carry_send,
    carry_recv,
    back_send,
    back_recv,
    sums_send,
    sums_recv,
    result_send,
    result_recv,
):
    ctx = lax.axis_index("ctx")
    x = lax.axis_index("tp")
    rows_y = lax.axis_size("ctx") // (2 * ZN)
    core = lax.rem(ctx, 2)
    z = lax.rem(ctx // 2, ZN)
    y = ctx // (2 * ZN)

    def device(dx, y_at, z_at, core_at):
        return (y_at * (2 * ZN) + z_at * 2 + core_at, lax.rem(x + dx, XN))

    sib = device(0, y, z, 1 - core)
    up = device(0, lax.rem(y + 1, rows_y), z, core)
    down = device(0, lax.rem(y + rows_y - 1, rows_y), z, core)
    ring = [lax.rem(z + d, ZN) for d in (4, 3, 5, 2, 6, 1, 7)]
    heads_of = [(2, 1), (2, 0), (1, 1), (3, 1), (1, 0), (3, 0), (0, 1)]
    cross = [
        (2 * lax.rem(x + dx, XN) + lax.rem(core + dc, 2), device(dx, y, z, lax.rem(core + dc, 2)))
        for dx, dc in heads_of
    ]

    def at_z(other):
        return device(0, y, other, core)

    barrier = pltpu.get_barrier_semaphore()
    partners = [at_z(other) for other in ring] + [up, down] + [target for _, target in cross]
    for partner in partners:
        pl.semaphore_signal(barrier, 1, device_id=partner, device_id_type=MESH)

    mine = pl.ds(pl.multiple_of(core * WIDE, WIDE), WIDE)
    theirs = pl.ds(pl.multiple_of((1 - core) * WIDE, WIDE), WIDE)
    own = pl.ds(pl.multiple_of(core * TOK, TOK), TOK)
    other_rows = pl.ds(pl.multiple_of((1 - core) * TOK, TOK), TOK)

    loads = [
        pltpu.make_async_copy(src, dst, local_sem.at[i])
        for i, (src, dst) in enumerate(
            (
                (k_hbm.at[:, theirs], k_other),
                (v_hbm.at[:, theirs], v_other),
                (k_hbm.at[:, mine], k.at[own]),
                (v_hbm.at[:, mine], v.at[own]),
                (slopes_hbm, slopes),
                (doc_hbm, doc_lengths),
                (gain_hbm, gain_flat),
                (q_hbm.at[:, mine], q.at[own]),
                (og_hbm.at[:, mine], og.at[own]),
            )
        )
    ]
    for load in loads:
        load.start()

    def remote(src, dst, send, recv, target):
        return pltpu.make_async_remote_copy(
            src_ref=src,
            dst_ref=dst,
            send_sem=send,
            recv_sem=recv,
            device_id=target,
            device_id_type=MESH,
        )

    swaps = [
        remote(src, dst.at[own], swap_send.at[i], swap_recv.at[i], sib)
        for i, (src, dst) in enumerate(
            ((k_other, k), (v_other, v), (q_hbm.at[:, theirs], q), (og_hbm.at[:, theirs], og))
        )
    ]

    for load in loads[4:7]:
        load.wait()

    starts = [jnp.int32(0)]
    for j in range(doc_lengths.shape[0] - 1):
        starts.append(starts[-1] + doc_lengths[j])

    def carries(block):
        hit = starts[0] == block
        for start in starts[1:]:
            hit = hit | (start == block)
        return jnp.where(hit, F32(0.0), F32(1.0))

    flag0 = carries(y * (2 * ZN) + 2 * z)
    flag1 = carries(y * (2 * ZN) + 2 * z + 1)
    slope = [slopes[HALF * core + i] for i in range(HALF)]
    for i in range(HALF):
        begin = pl.multiple_of(core * WIDE + i * HD, HD)
        gain[:, i * HD : (i + 1) * HD] = gain_flat[pl.ds(begin, HD)].reshape(1, HD)

    token = lax.broadcasted_iota(jnp.int32, (PAIR, HD), 0)
    second = token >= TOK
    token_f = token.astype(F32)
    entry_flag = jnp.where(second, flag0 * flag1, flag0)
    tail_flag = jnp.where(second, 1.0, flag1)

    def entry(i):
        return jnp.exp(-slope[i] * (token_f + 1.0)) * entry_flag

    def tail(i):
        return jnp.exp(-slope[i] * (PAIR - 1.0 - token_f)) * tail_flag

    def cols(i):
        return slice(i * HD, (i + 1) * HD)

    row = lax.broadcasted_iota(jnp.int32, (PAIR, PAIR), 0)
    column = lax.broadcasted_iota(jnp.int32, (PAIR, PAIR), 1)
    distance = (row - column).astype(F32)
    reach = jnp.where((row >= TOK) & (column < TOK), flag1, 1.0)
    for i in range(HALF):
        table[i] = jnp.where(
            distance >= 0.0, jnp.exp(-slope[i] * jnp.maximum(distance, 0.0)) * reach, 0.0
        )

    share_slope = slopes[HALF * core + z // PER]
    lam2 = jnp.exp(jnp.full((1, HD), -1.0 * PAIR, F32) * share_slope)
    step_decay = [
        lam2 * (carries(y * (2 * ZN) + 2 * j) * carries(y * (2 * ZN) + 2 * j + 1))
        for j in range(ZN)
    ]

    def scan(phase, backward):
        sends = []
        for other in ring:
            copy = remote(
                share_out.at[phase, other],
                share_in.at[phase, z],
                share_send.at[phase, other],
                share_recv.at[phase, z],
                at_z(other),
            )
            copy.start()
            sends.append(copy)
        share_in[phase, z] = share_out[phase, z]

        yield

        for other in ring[::-1]:
            remote(
                share_out.at[phase, z],
                share_in.at[phase, other],
                share_send.at[phase, other],
                share_recv.at[phase, other],
                at_z(other),
            ).wait_recv()
        order = range(ZN - 1, -1, -1) if backward else range(ZN)
        total = jnp.zeros((SHARE, HD), F32)
        product = jnp.ones((1, HD), F32)
        before, products = {}, {}
        for j in order:
            before[j], products[j] = total, product
            total = total * step_decay[j] + share_in[phase, j].astype(F32)
            product = product * step_decay[j]
        carry_out[phase] = total.astype(BF16)
        carry = remote(
            carry_out.at[phase],
            carry_in.at[phase],
            carry_send.at[phase],
            carry_recv.at[phase],
            down if backward else up,
        )
        carry.start()
        carry.wait_recv()
        incoming = carry_in[phase].astype(F32)
        for j in range(ZN):
            back_out[phase, j] = (before[j] + products[j] * incoming).astype(BF16)
        for other in ring:
            copy = remote(
                back_out.at[phase, other],
                back_in.at[phase, z],
                back_send.at[phase, other],
                back_recv.at[phase, z],
                at_z(other),
            )
            copy.start()
            sends.append(copy)
        back_in[phase, z] = back_out[phase, z]

        yield

        for other in ring[::-1]:
            remote(
                back_out.at[phase, z],
                back_in.at[phase, other],
                back_send.at[phase, other],
                back_recv.at[phase, other],
                at_z(other),
            ).wait_recv()
        for copy in sends:
            copy.wait_send()
        carry.wait_send()
        yield

    def state(phase, i):
        return jnp.concatenate([back_in[phase, PER * i + j] for j in range(PER)], axis=0)

    def put_shares(phase, i, value):
        for j in range(PER):
            share_out[phase, PER * i + j] = value[j * SHARE : (j + 1) * SHARE].astype(BF16)

    loads[0].wait()
    loads[1].wait()
    pl.semaphore_wait(barrier, len(partners))
    for swap in swaps:
        swap.start()
    loads[2].wait()
    loads[3].wait()
    swaps[0].wait_recv()
    swaps[1].wait_recv()
    for i in range(HALF):
        value_decayed = (tail(i) * v[:, cols(i)].astype(F32)).astype(BF16)
        put_shares(0, i, dot(k[:, cols(i)], value_decayed, 0, 0))
    forward = scan(0, False)
    next(forward)

    loads[7].wait()
    loads[8].wait()
    swaps[2].wait_recv()
    swaps[3].wait_recv()
    for i in range(HALF):
        weight = (dot(q[:, cols(i)], k[:, cols(i)], 1, 1) * table[i]).astype(BF16)
        weights[i] = weight
        raw[:, cols(i)] = dot(weight, v[:, cols(i)], 1, 0)

    next(forward)
    next(forward)
    squares = jnp.zeros((PAIR, HD), F32)
    products = jnp.zeros((PAIR, HD), F32)
    for i in range(HALF):
        raw_i = raw[:, cols(i)] + dot(q[:, cols(i)], state(0, i), 1, 0) * entry(i)
        raw[:, cols(i)] = raw_i
        squares = squares + raw_i * raw_i
        products = products + raw_i * (og[:, cols(i)].astype(F32) * gain[:, cols(i)])

    def token_row(values):
        return jnp.sum(values.T, axis=0, keepdims=True)

    place = lax.broadcasted_iota(jnp.int32, (8, HD), 0)
    slot = 2 * x + core
    sums[slot] = jnp.where(
        place < 4,
        jnp.where(place < 2, token_row(squares[:TOK]), token_row(squares[TOK:])),
        jnp.where(place < 6, token_row(products[:TOK]), token_row(products[TOK:])),
    )
    sum_copies = []
    for index, target in cross:
        copy = remote(
            sums.at[slot], sums.at[slot], sums_send.at[index], sums_recv.at[slot], target
        )
        copy.start()
        sum_copies.append(copy)
    for index, target in cross[::-1]:
        remote(
            sums.at[slot], sums.at[index], sums_send.at[index], sums_recv.at[index], target
        ).wait_recv()
    total = sums[0]
    for j in range(1, 2 * XN):
        total = total + sums[j]
    inverse_rows = lax.rsqrt(total[0:4] / features + EPSILON)
    factor_rows = inverse_rows * inverse_rows * inverse_rows * total[4:8] / features

    def token_columns(rows):
        return jnp.concatenate(
            [jnp.broadcast_to(rows[j : j + 1], (HD, HD)).T for j in (0, 2)], axis=0
        )

    inverse = token_columns(inverse_rows)
    factor = token_columns(factor_rows)

    for i in range(HALF):
        scaled = og[:, cols(i)].astype(F32) * gain[:, cols(i)]
        grad = (inverse * scaled - factor * raw[:, cols(i)]).astype(BF16)
        og[:, cols(i)] = grad
        query_decayed = (entry(i) * q[:, cols(i)].astype(F32)).astype(BF16)
        put_shares(1, i, dot(query_decayed, grad, 0, 0))
    backward = scan(1, True)
    next(backward)

    results = []

    def deliver(source, target):
        j = len(results) // 2
        keep = pltpu.make_async_copy(source.at[own], target.at[:, mine], own_sem.at[j])
        send = remote(
            source.at[other_rows], target.at[:, mine], result_send.at[j], result_recv.at[j], sib
        )
        send.start()
        keep.start()
        results.extend((keep, send))

    for i in range(HALF):
        att[:, cols(i)] = (raw[:, cols(i)] * inverse * gain[:, cols(i)]).astype(BF16)
    deliver(att, att_out)
    for i in range(HALF):
        grad = og[:, cols(i)]
        dscore = (dot(grad, v[:, cols(i)], 1, 1) * table[i]).astype(BF16)
        dq[:, cols(i)] = (
            dot(dscore, k[:, cols(i)], 1, 0) + dot(grad, state(0, i), 1, 1) * entry(i)
        ).astype(BF16)
        dk_part[:, cols(i)] = dot(dscore, q[:, cols(i)], 0, 0)
        dv_part[:, cols(i)] = dot(weights[i], grad, 0, 0)
    deliver(dq, dq_out)

    next(backward)
    next(backward)
    for i in range(HALF):
        dk[:, cols(i)] = (
            dk_part[:, cols(i)] + dot(v[:, cols(i)], state(1, i), 1, 1) * tail(i)
        ).astype(BF16)
    deliver(dk, dk_out)
    for i in range(HALF):
        dv[:, cols(i)] = (
            dv_part[:, cols(i)] + dot(k[:, cols(i)], state(1, i), 1, 0) * tail(i)
        ).astype(BF16)
    deliver(dv, dv_out)

    for swap in swaps:
        swap.wait_send()
    for copy in sum_copies:
        copy.wait_send()
    for copy in results:
        copy.wait()


def place_results(*refs):
    sources, targets, sems = refs[:4], refs[4:8], refs[8]
    copies = [
        pltpu.make_async_copy(src, dst, sems.at[i])
        for i, (src, dst) in enumerate(zip(sources, targets))
    ]
    for copy in copies:
        copy.start()
    for copy in copies:
        copy.wait()


def body(query_rows, key_rows, value_rows, out_grad, slopes, norm_gain, doc_lengths):
    rows, width = query_rows.shape
    features = width * lax.axis_size("tp")
    whole = jax.ShapeDtypeStruct((rows, width), BF16)
    in_hbm = pl.BlockSpec(memory_space=pltpu.HBM)
    in_vmem = pl.BlockSpec(memory_space=pltpu.VMEM)
    dma = pltpu.SemaphoreType.DMA
    pair_bf16 = pltpu.VMEM((PAIR, WIDE), BF16)
    pair_f32 = pltpu.VMEM((PAIR, WIDE), F32)
    shares = pltpu.VMEM((2, ZN, SHARE, HD), BF16)
    carry = pltpu.VMEM((2, SHARE, HD), BF16)
    results = pl.pallas_call(
        functools.partial(kernel, features),
        out_shape=(pltpu.VMEM((rows, width), BF16),) * 4,
        in_specs=[in_hbm] * 7,
        out_specs=(in_vmem,) * 4,
        scratch_shapes=[
            pltpu.SMEM(slopes.shape, F32),
            pltpu.SMEM(doc_lengths.shape, jnp.int32),
            pltpu.VMEM((width,), F32),
            pltpu.VMEM((1, WIDE), F32),
            pair_bf16,
            pair_bf16,
            pair_bf16,
            pair_bf16,
            pltpu.VMEM((TOK, WIDE), BF16),
            pltpu.VMEM((TOK, WIDE), BF16),
            pair_bf16,
            pair_bf16,
            pair_bf16,
            pair_bf16,
            pltpu.VMEM((HALF, PAIR, PAIR), F32),
            pltpu.VMEM((HALF, PAIR, PAIR), BF16),
            pair_f32,
            pair_f32,
            pair_f32,
            shares,
            shares,
            carry,
            carry,
            shares,
            shares,
            pltpu.VMEM((2 * XN, 8, HD), F32),
            dma((9,)),
            dma((4,)),
            dma((4,)),
            dma((4,)),
            dma((2, ZN)),
            dma((2, ZN)),
            dma((2,)),
            dma((2,)),
            dma((2, ZN)),
            dma((2, ZN)),
            dma((2 * XN,)),
            dma((2 * XN,)),
            dma((4,)),
            dma((4,)),
        ],
        compiler_params=pltpu.CompilerParams(
            collective_id=0, has_side_effects=True, vmem_limit_bytes=48 * 1024 * 1024
        ),
        name="lightning",
    )(
        *(
            pltpu.with_memory_space_constraint(a, pltpu.HBM)
            for a in (slopes, doc_lengths, query_rows, key_rows, value_rows, out_grad, norm_gain)
        )
    )
    return pl.pallas_call(
        place_results,
        out_shape=(whole,) * 4,
        in_specs=[in_vmem] * 4,
        out_specs=(in_hbm,) * 4,
        scratch_shapes=[dma((4,))],
        name="place",
    )(*results)


def solution(mesh):
    spec = P("ctx", "tp")
    in_specs = (spec, spec, spec, spec, P("tp"), P("tp"), P())
    return jax.shard_map(
        body, mesh=mesh, in_specs=in_specs, out_specs=(spec,) * 4, check_vma=False
    )
```

time: 84.2 us -> 54.7 us (0.65)
  Pallas kernels: 83.4 us -> 51.1 us
  local copies, waits for them, and re-layouts: 0 us -> 2.78 us
    pallas_call x2, Pallas kernels: 83.4 us -> 51.1 us  [the longest x1 49 us: body(): pl.pallas_call(functools.partial(kernel, features), out_shape=(pltpu.VMEM...]
    unnamed x0 -> x8, local copies, waits for them, and re-layouts: none -> 2.78 us
where the time goes in v2:
time: 54.7 us; the launch traced here: 54.6 us
  Pallas kernels  51.1 us (93%)
  local copies, waits for them, and re-layouts  2.78 us (5%)
  between operations  0.65 us (1%)
    pallas_call x1, Pallas kernels, body(): pl.pallas_call(functools.partial(kernel, features), out_shape=(pltpu.VMEM...  49 us
    unnamed x8, local copies, waits for them, and re-layouts  2.78 us
    pallas_call x1, Pallas kernels, body(): pl.pallas_call(place_results, out_shape=(whole,) * 4, in_specs=[in_vmem]...  2.18 us

profile of v2, /device:TPU:1, one launch (start us, length us, event | category | flops | bytes accessed | tf_op | source)
XLA Modules:
  0.0 54.6 jit_solution(10314429363403475056)
XLA Ops:
  0.6 49.0 %lightning.1 = (bf16[128,1024]{1,0:T(8,128)(2,1)S(1)}, bf16[128,1024]{1,0:T(8,128)(2,1)S(1)}, bf16[128,1024]{1,0:T(8,128)(2,1)S(1)}, bf16[128,1024]{1,0:T(8,128)(2,1)S(1)}) custom-call(f32[8]{0:T(128)} %slopes_hbm.1, s32[16]{0:T(128)} %doc_hbm.1, bf16[128,1024]{1,0:T(8,128)(2,1)} %q_hbm.1, bf16[128,1024]{1,0:T(8,128)(2,1)} %k_hbm.1, ...), custom_call_target="tpu_custom_call" | custom-call | tf_op jit(solution)/shard_map/lightning/pallas_call | solution.py:429
  49.6 0.0 copy-start
  49.6 0.7 %copy-done = bf16[128,1024]{1,0:T(8,128)(2,1)} copy-done((bf16[128,1024]{1,0:T(8,128)(2,1)}, bf16[128,1024]{1,0:T(8,128)(2,1)S(1)}, u32[]{:S(2)}) %copy-start) | copy-done | bytes 262168
  50.3 0.0 copy-start.1
  50.3 0.7 %copy-done.1 = bf16[128,1024]{1,0:T(8,128)(2,1)} copy-done((bf16[128,1024]{1,0:T(8,128)(2,1)}, bf16[128,1024]{1,0:T(8,128)(2,1)S(1)}, u32[]{:S(2)}) %copy-start.1) | copy-done | bytes 262168
  51.0 0.0 copy-start.2
  51.0 0.7 %copy-done.2 = bf16[128,1024]{1,0:T(8,128)(2,1)} copy-done((bf16[128,1024]{1,0:T(8,128)(2,1)}, bf16[128,1024]{1,0:T(8,128)(2,1)S(1)}, u32[]{:S(2)}) %copy-start.2) | copy-done | bytes 262168
  51.7 0.0 copy-start.3
  51.7 0.7 %copy-done.3 = bf16[128,1024]{1,0:T(8,128)(2,1)} copy-done((bf16[128,1024]{1,0:T(8,128)(2,1)}, bf16[128,1024]{1,0:T(8,128)(2,1)S(1)}, u32[]{:S(2)}) %copy-start.3) | copy-done | bytes 262168
  52.4 2.2 %place.1 = (bf16[128,1024]{1,0:T(8,128)(2,1)}, bf16[128,1024]{1,0:T(8,128)(2,1)}, bf16[128,1024]{1,0:T(8,128)(2,1)}, bf16[128,1024]{1,0:T(8,128)(2,1)}) custom-call(bf16[128,1024]{1,0:T(8,128)(2,1)} %copy-done, bf16[128,1024]{1,0:T(8,128)(2,1)} %copy-done.1, bf16[128,1024]{1,0:T(8,128)(2,1)} %copy-done.2, bf16[128,1024]{1,0:T(8,128)(2,1)} %copy-done.3), custom_call_target="tpu_custom_call" | custom-call | tf_op jit(solution)/shard_map/place/pallas_call | solution.py:486
Async XLA Ops:
  49.6 0.7 %copy-start = (bf16[128,1024]{1,0:T(8,128)(2,1)}, bf16[128,1024]{1,0:T(8,128)(2,1)S(1)}, u32[]{:S(2)}) copy-start(bf16[128,1024]{1,0:T(8,128)(2,1)S(1)} %get-tuple-element.8.refs_0_) | copy-start | bytes 786436
  50.3 0.7 %copy-start.1 = (bf16[128,1024]{1,0:T(8,128)(2,1)}, bf16[128,1024]{1,0:T(8,128)(2,1)S(1)}, u32[]{:S(2)}) copy-start(bf16[128,1024]{1,0:T(8,128)(2,1)S(1)} %get-tuple-element.9.refs_1_) | copy-start | bytes 786436
  51.0 0.7 %copy-start.2 = (bf16[128,1024]{1,0:T(8,128)(2,1)}, bf16[128,1024]{1,0:T(8,128)(2,1)S(1)}, u32[]{:S(2)}) copy-start(bf16[128,1024]{1,0:T(8,128)(2,1)S(1)} %get-tuple-element.10.refs_2_) | copy-start | bytes 786436
  51.7 0.7 %copy-start.3 = (bf16[128,1024]{1,0:T(8,128)(2,1)}, bf16[128,1024]{1,0:T(8,128)(2,1)S(1)}, u32[]{:S(2)}) copy-start(bf16[128,1024]{1,0:T(8,128)(2,1)S(1)} %get-tuple-element.11.refs_3_) | copy-start | bytes 786436

commit v3 on v2

--- a/solution.py
+++ b/solution.py
@@ -51,8 +51,12 @@
     v_other,
     att,
     dq,
-    dk,
-    dv,
+    last,
+    entries,
+    tails,
+    local,
+    local_other,
+    local_in,
     table,
     weights,
     raw,
@@ -79,6 +83,8 @@
     sums_recv,
     result_send,
     result_recv,
+    last_send,
+    last_recv,
 ):
     ctx = lax.axis_index("ctx")
     x = lax.axis_index("tp")
@@ -148,6 +154,7 @@
             ((k_other, k), (v_other, v), (q_hbm.at[:, theirs], q), (og_hbm.at[:, theirs], og))
         )
     ]
+    state_swap = remote(local_other, local_in, swap_send.at[4], swap_recv.at[4], sib)
 
     for load in loads[4:7]:
         load.wait()
@@ -169,29 +176,38 @@
         begin = pl.multiple_of(core * WIDE + i * HD, HD)
         gain[:, i * HD : (i + 1) * HD] = gain_flat[pl.ds(begin, HD)].reshape(1, HD)
 
-    token = lax.broadcasted_iota(jnp.int32, (PAIR, HD), 0)
-    second = token >= TOK
-    token_f = token.astype(F32)
-    entry_flag = jnp.where(second, flag0 * flag1, flag0)
-    tail_flag = jnp.where(second, 1.0, flag1)
-
-    def entry(i):
-        return jnp.exp(-slope[i] * (token_f + 1.0)) * entry_flag
-
-    def tail(i):
-        return jnp.exp(-slope[i] * (PAIR - 1.0 - token_f)) * tail_flag
-
     def cols(i):
-        return slice(i * HD, (i + 1) * HD)
-
-    row = lax.broadcasted_iota(jnp.int32, (PAIR, PAIR), 0)
-    column = lax.broadcasted_iota(jnp.int32, (PAIR, PAIR), 1)
-    distance = (row - column).astype(F32)
-    reach = jnp.where((row >= TOK) & (column < TOK), flag1, 1.0)
-    for i in range(HALF):
-        table[i] = jnp.where(
-            distance >= 0.0, jnp.exp(-slope[i] * jnp.maximum(distance, 0.0)) * reach, 0.0
-        )
+        return pl.ds(pl.multiple_of(i * HD, HD), HD)
+
+    is0 = core == 0
+    to_end = (TOK - 1.0) - lax.broadcasted_iota(jnp.int32, (TOK, HD), 0).astype(F32)
+    to_end = to_end + jnp.where(is0, F32(TOK), F32(0.0))
+    end_flag = jnp.where(is0, flag1, F32(1.0))
+
+    def local_state(keys, values, head):
+        kept = jnp.exp(-slopes[head] * to_end) * end_flag
+        return dot(keys, (kept * values.astype(F32)).astype(BF16), 0, 0)
+
+    loads[0].wait()
+    loads[1].wait()
+    for i in range(HALF):
+        local_other[i] = local_state(
+            k_other[:, cols(i)], v_other[:, cols(i)], HALF * (1 - core) + i
+        ).astype(BF16)
+    loads[2].wait()
+    loads[3].wait()
+    for i in range(HALF):
+        local[i] = local_state(k[own, cols(i)], v[own, cols(i)], HALF * core + i)
+
+    far = lax.rem(z // PER + HALF // 2, HALF)
+    near = z // PER
+    between = [lax.rem(far + d, HALF) for d in (1, 3)]
+    next_door = z + 1 - 2 * lax.rem(z, 2)
+    send_order = [far] + between + [near]
+    use_order = [near] + between[::-1] + [far]
+
+    def shares_of(i):
+        return [next_door] if i is near else [PER * i + j for j in range(PER)]
 
     share_slope = slopes[HALF * core + z // PER]
     lam2 = jnp.exp(jnp.full((1, HD), -1.0 * PAIR, F32) * share_slope)
@@ -200,22 +216,32 @@
         for j in range(ZN)
     ]
 
-    def scan(phase, backward):
-        sends = []
-        for other in ring:
-            copy = remote(
-                share_out.at[phase, other],
-                share_in.at[phase, z],
-                share_send.at[phase, other],
-                share_recv.at[phase, z],
-                at_z(other),
-            )
-            copy.start()
-            sends.append(copy)
-        share_in[phase, z] = share_out[phase, z]
-
-        yield
-
+    def share_copy(phase, other):
+        return remote(
+            share_out.at[phase, other],
+            share_in.at[phase, z],
+            share_send.at[phase, other],
+            share_recv.at[phase, z],
+            at_z(other),
+        )
+
+    def back_copy(phase, other):
+        return remote(
+            back_out.at[phase, other],
+            back_in.at[phase, z],
+            back_send.at[phase, other],
+            back_recv.at[phase, z],
+            at_z(other),
+        )
+
+    def send_shares(phase, i, value):
+        share_out[phase, pl.ds(PER * i, PER)] = value.astype(BF16).reshape(PER, SHARE, HD)
+        for other in shares_of(i):
+            share_copy(phase, other).start()
+        if i is near:
+            share_in[phase, z] = share_out[phase, z]
+
+    def turn(phase, backward):
         for other in ring[::-1]:
             remote(
                 share_out.at[phase, z],
@@ -246,20 +272,14 @@
         for j in range(ZN):
             back_out[phase, j] = (before[j] + products[j] * incoming).astype(BF16)
         for other in ring:
-            copy = remote(
-                back_out.at[phase, other],
-                back_in.at[phase, z],
-                back_send.at[phase, other],
-                back_recv.at[phase, z],
-                at_z(other),
-            )
-            copy.start()
-            sends.append(copy)
+            back_copy(phase, other).start()
         back_in[phase, z] = back_out[phase, z]
-
-        yield
-
-        for other in ring[::-1]:
+        for other in ring:
+            share_copy(phase, other).wait_send()
+        carry.wait_send()
+
+    def arrived(phase, i):
+        for other in shares_of(i):
             remote(
                 back_out.at[phase, z],
                 back_in.at[phase, other],
@@ -267,48 +287,48 @@
                 back_recv.at[phase, other],
                 at_z(other),
             ).wait_recv()
-        for copy in sends:
-            copy.wait_send()
-        carry.wait_send()
-        yield
+        return state(phase, i)
 
     def state(phase, i):
-        return jnp.concatenate([back_in[phase, PER * i + j] for j in range(PER)], axis=0)
-
-    def put_shares(phase, i, value):
-        for j in range(PER):
-            share_out[phase, PER * i + j] = value[j * SHARE : (j + 1) * SHARE].astype(BF16)
-
-    loads[0].wait()
-    loads[1].wait()
+        return back_in[phase, pl.ds(PER * i, PER)].reshape(HD, HD)
+
     pl.semaphore_wait(barrier, len(partners))
+    state_swap.start()
+    state_swap.wait_recv()
+    for i in send_order:
+        send_shares(0, i, local[i] + local_in[i].astype(F32))
     for swap in swaps:
         swap.start()
-    loads[2].wait()
-    loads[3].wait()
-    swaps[0].wait_recv()
-    swaps[1].wait_recv()
-    for i in range(HALF):
-        value_decayed = (tail(i) * v[:, cols(i)].astype(F32)).astype(BF16)
-        put_shares(0, i, dot(k[:, cols(i)], value_decayed, 0, 0))
-    forward = scan(0, False)
-    next(forward)
-
-    loads[7].wait()
-    loads[8].wait()
-    swaps[2].wait_recv()
-    swaps[3].wait_recv()
+
+    token = lax.broadcasted_iota(jnp.int32, (PAIR, HD), 0)
+    second = token >= TOK
+    token_f = token.astype(F32)
+    entry_flag = jnp.where(second, flag0 * flag1, flag0)
+    tail_flag = jnp.where(second, 1.0, flag1)
+    row = lax.broadcasted_iota(jnp.int32, (PAIR, PAIR), 0)
+    column = lax.broadcasted_iota(jnp.int32, (PAIR, PAIR), 1)
+    distance = (row - column).astype(F32)
+    reach = jnp.where((row >= TOK) & (column < TOK), flag1, 1.0)
+    for i in range(HALF):
+        entries[i] = jnp.exp(-slope[i] * (token_f + 1.0)) * entry_flag
+        tails[i] = jnp.exp(-slope[i] * (PAIR - 1.0 - token_f)) * tail_flag
+        table[i] = jnp.where(
+            distance >= 0.0, jnp.exp(-slope[i] * jnp.maximum(distance, 0.0)) * reach, 0.0
+        )
+    for load in loads[7:]:
+        load.wait()
+    for swap in swaps:
+        swap.wait_recv()
     for i in range(HALF):
         weight = (dot(q[:, cols(i)], k[:, cols(i)], 1, 1) * table[i]).astype(BF16)
         weights[i] = weight
         raw[:, cols(i)] = dot(weight, v[:, cols(i)], 1, 0)
 
-    next(forward)
-    next(forward)
+    turn(0, False)
     squares = jnp.zeros((PAIR, HD), F32)
     products = jnp.zeros((PAIR, HD), F32)
-    for i in range(HALF):
-        raw_i = raw[:, cols(i)] + dot(q[:, cols(i)], state(0, i), 1, 0) * entry(i)
+    for i in use_order:
+        raw_i = raw[:, cols(i)] + dot(q[:, cols(i)], arrived(0, i), 1, 0) * entries[i]
         raw[:, cols(i)] = raw_i
         squares = squares + raw_i * raw_i
         products = products + raw_i * (og[:, cols(i)].astype(F32) * gain[:, cols(i)])
@@ -348,14 +368,12 @@
     inverse = token_columns(inverse_rows)
     factor = token_columns(factor_rows)
 
-    for i in range(HALF):
+    for i in send_order:
         scaled = og[:, cols(i)].astype(F32) * gain[:, cols(i)]
         grad = (inverse * scaled - factor * raw[:, cols(i)]).astype(BF16)
         og[:, cols(i)] = grad
-        query_decayed = (entry(i) * q[:, cols(i)].astype(F32)).astype(BF16)
-        put_shares(1, i, dot(query_decayed, grad, 0, 0))
-    backward = scan(1, True)
-    next(backward)
+        query_decayed = (entries[i] * q[:, cols(i)].astype(F32)).astype(BF16)
+        send_shares(1, i, dot(query_decayed, grad, 0, 0))
 
     results = []
 
@@ -376,30 +394,46 @@
         grad = og[:, cols(i)]
         dscore = (dot(grad, v[:, cols(i)], 1, 1) * table[i]).astype(BF16)
         dq[:, cols(i)] = (
-            dot(dscore, k[:, cols(i)], 1, 0) + dot(grad, state(0, i), 1, 1) * entry(i)
+            dot(dscore, k[:, cols(i)], 1, 0) + dot(grad, state(0, i), 1, 1) * entries[i]
         ).astype(BF16)
         dk_part[:, cols(i)] = dot(dscore, q[:, cols(i)], 0, 0)
         dv_part[:, cols(i)] = dot(weights[i], grad, 0, 0)
     deliver(dq, dq_out)
 
-    next(backward)
-    next(backward)
-    for i in range(HALF):
-        dk[:, cols(i)] = (
-            dk_part[:, cols(i)] + dot(v[:, cols(i)], state(1, i), 1, 1) * tail(i)
-        ).astype(BF16)
-    deliver(dk, dk_out)
-    for i in range(HALF):
-        dv[:, cols(i)] = (
-            dv_part[:, cols(i)] + dot(k[:, cols(i)], state(1, i), 1, 0) * tail(i)
-        ).astype(BF16)
-    deliver(dv, dv_out)
-
-    for swap in swaps:
+    turn(1, True)
+
+    def finish(j, i, value, target):
+        value = value.astype(BF16)
+        place_at = pl.ds(pl.multiple_of(core * WIDE + i * HD, HD), HD)
+        target[:, place_at] = jnp.where(is0, value[:TOK], value[TOK:])
+        last[j, i] = jnp.where(is0, value[TOK:], value[:TOK])
+        return remote(
+            last.at[j, i], target.at[:, place_at], last_send.at[j, i], last_recv.at[j, i], sib
+        )
+
+    finals = []
+    for i in use_order:
+        grad_state = arrived(1, i)
+        for j, (part, operand, side, target) in enumerate(
+            ((dk_part, v, 1, dk_out), (dv_part, k, 0, dv_out))
+        ):
+            copy = finish(
+                j,
+                i,
+                part[:, cols(i)] + dot(operand[:, cols(i)], grad_state, 1, side) * tails[i],
+                target,
+            )
+            copy.start()
+            finals.append(copy)
+
+    for swap in swaps + [state_swap]:
         swap.wait_send()
     for copy in sum_copies:
         copy.wait_send()
-    for copy in results:
+    for phase in range(2):
+        for other in ring:
+            back_copy(phase, other).wait_send()
+    for copy in results + finals:
         copy.wait()
 
 
@@ -444,8 +478,12 @@
             pltpu.VMEM((TOK, WIDE), BF16),
             pair_bf16,
             pair_bf16,
-            pair_bf16,
-            pair_bf16,
+            pltpu.VMEM((2, HALF, TOK, HD), BF16),
+            pltpu.VMEM((HALF, PAIR, HD), F32),
+            pltpu.VMEM((HALF, PAIR, HD), F32),
+            pltpu.VMEM((HALF, HD, HD), F32),
+            pltpu.VMEM((HALF, HD, HD), BF16),
+            pltpu.VMEM((HALF, HD, HD), BF16),
             pltpu.VMEM((HALF, PAIR, PAIR), F32),
             pltpu.VMEM((HALF, PAIR, PAIR), BF16),
             pair_f32,
@@ -459,9 +497,9 @@
             shares,
             pltpu.VMEM((2 * XN, 8, HD), F32),
             dma((9,)),
-            dma((4,)),
-            dma((4,)),
-            dma((4,)),
+            dma((2,)),
+            dma((5,)),
+            dma((5,)),
             dma((2, ZN)),
             dma((2, ZN)),
             dma((2,)),
@@ -470,8 +508,10 @@
             dma((2, ZN)),
             dma((2 * XN,)),
             dma((2 * XN,)),
-            dma((4,)),
-            dma((4,)),
+            dma((2,)),
+            dma((2,)),
+            dma((2, HALF)),
+            dma((2, HALF)),
         ],
         compiler_params=pltpu.CompilerParams(
             collective_id=0, has_side_effects=True, vmem_limit_bytes=48 * 1024 * 1024
@@ -489,8 +529,9 @@
         in_specs=[in_vmem] * 4,
         out_specs=(in_hbm,) * 4,
         scratch_shapes=[dma((4,))],
+        compiler_params=pltpu.CompilerParams(vmem_limit_bytes=8 * 1024 * 1024),
         name="place",
-    )(*results)
+    )(*(pltpu.with_memory_space_constraint(a, pltpu.VMEM) for a in results))
 
 
 def solution(mesh):

time: 54.7 us -> 50.6 us (0.925)
  local copies, waits for them, and re-layouts: 2.78 us -> 0 us
  Pallas kernels: 51.1 us -> 49.8 us
    unnamed x8 -> x0, local copies, waits for them, and re-layouts: 2.78 us -> none
    pallas_call x1, Pallas kernels: 2.18 us -> 1 us  [body(): pl.pallas_call(place_results, out_shape=(whole,) * 4, in_specs=[in_vmem]...]
where the time goes in v3:
time: 50.6 us; the launch traced here: 50.4 us
  Pallas kernels  49.8 us (98%)
  between operations  0.64 us (1%)
    pallas_call x1, Pallas kernels, body(): pl.pallas_call(functools.partial(kernel, features), out_shape=(pltpu.VMEM...  48.8 us

profile of v3, /device:TPU:1, one launch (start us, length us, event | category | flops | bytes accessed | tf_op | source)
XLA Modules:
  0.0 50.4 jit_solution(9084080968872782440)
XLA Ops:
  0.6 48.8 %lightning.1 = (bf16[128,1024]{1,0:T(8,128)(2,1)S(1)}, bf16[128,1024]{1,0:T(8,128)(2,1)S(1)}, bf16[128,1024]{1,0:T(8,128)(2,1)S(1)}, bf16[128,1024]{1,0:T(8,128)(2,1)S(1)}) custom-call(f32[8]{0:T(128)} %slopes_hbm.1, s32[16]{0:T(128)} %doc_hbm.1, bf16[128,1024]{1,0:T(8,128)(2,1)} %q_hbm.1, bf16[128,1024]{1,0:T(8,128)(2,1)} %k_hbm.1, ...), custom_call_target="tpu_custom_call" | custom-call | tf_op jit(solution)/shard_map/lightning/pallas_call | solution.py:463
  49.4 1.0 %place.1 = (bf16[128,1024]{1,0:T(8,128)(2,1)}, bf16[128,1024]{1,0:T(8,128)(2,1)}, bf16[128,1024]{1,0:T(8,128)(2,1)}, bf16[128,1024]{1,0:T(8,128)(2,1)}) custom-call(bf16[128,1024]{1,0:T(8,128)(2,1)S(1)} %get-tuple-element.8.refs_0_, bf16[128,1024]{1,0:T(8,128)(2,1)S(1)} %get-tuple-element.9.refs_1_, bf16[128,1024]{1,0:T(8,128)(2,1)S(1)} %get-tuple-element.10.refs_2_, ...), custom_call_target="tpu_custom_call" | custom-call | tf_op jit(solution)/shard_map/place/pallas_call | solution.py:526

commit v4 on v3

--- a/solution.py
+++ b/solution.py
@@ -69,6 +69,7 @@
     back_out,
     back_in,
     sums,
+    answers,
     local_sem,
     own_sem,
     swap_send,
@@ -97,8 +98,6 @@
         return (y_at * (2 * ZN) + z_at * 2 + core_at, lax.rem(x + dx, XN))
 
     sib = device(0, y, z, 1 - core)
-    up = device(0, lax.rem(y + 1, rows_y), z, core)
-    down = device(0, lax.rem(y + rows_y - 1, rows_y), z, core)
     ring = [lax.rem(z + d, ZN) for d in (4, 3, 5, 2, 6, 1, 7)]
     heads_of = [(2, 1), (2, 0), (1, 1), (3, 1), (1, 0), (3, 0), (0, 1)]
     cross = [
@@ -106,13 +105,17 @@
         for dx, dc in heads_of
     ]
 
+    next_y, last_y = lax.rem(y + 1, rows_y), lax.rem(y + rows_y - 1, rows_y)
+
     def at_z(other):
         return device(0, y, other, core)
 
-    barrier = pltpu.get_barrier_semaphore()
-    partners = [at_z(other) for other in ring] + [up, down] + [target for _, target in cross]
-    for partner in partners:
-        pl.semaphore_signal(barrier, 1, device_id=partner, device_id_type=MESH)
+    def above(other):
+        return device(0, next_y, other, core)
+
+    def below(other):
+        return device(0, last_y, other, core)
+
 
     mine = pl.ds(pl.multiple_of(core * WIDE, WIDE), WIDE)
     theirs = pl.ds(pl.multiple_of((1 - core) * WIDE, WIDE), WIDE)
@@ -125,18 +128,52 @@
             (
                 (k_hbm.at[:, theirs], k_other),
                 (v_hbm.at[:, theirs], v_other),
+                (slopes_hbm, slopes),
+                (doc_hbm, doc_lengths),
                 (k_hbm.at[:, mine], k.at[own]),
                 (v_hbm.at[:, mine], v.at[own]),
-                (slopes_hbm, slopes),
-                (doc_hbm, doc_lengths),
                 (gain_hbm, gain_flat),
                 (q_hbm.at[:, mine], q.at[own]),
                 (og_hbm.at[:, mine], og.at[own]),
             )
         )
     ]
-    for load in loads:
+    for load in loads[:4]:
         load.start()
+
+    barrier = pltpu.get_barrier_semaphore()
+    along_z = [(other, at_z(other)) for other in ring]
+    along_y = [(next_y, above(z)), (last_y, below(z))]
+    along_x = [(index // 2, target) for index, target in cross[:-1]]
+
+    def signal_if(condition, semaphore, target):
+        @pl.when(condition)
+        def _():
+            pl.semaphore_signal(semaphore, 1, device_id=target, device_id_type=MESH)
+
+    pl.semaphore_signal(barrier, 1, device_id=sib, device_id_type=MESH)
+    for here, partners in ((z, along_z), (y, along_y), (x, along_x)):
+        for other, target in partners:
+            signal_if(other > here, barrier, target)
+    lower_y = (next_y < y).astype(jnp.int32) + (last_y < y).astype(jnp.int32)
+    greetings = 1 + z + lower_y + 2 * x
+
+    def wait_some(semaphore, count):
+        @pl.when(count > 0)
+        def _():
+            pl.semaphore_wait(semaphore, count)
+
+    def answer():
+        for other, target in along_z:
+            signal_if(other < z, answers.at[z], target)
+        for axis, here, partners in ((ZN, y, along_y), (ZN + 1, x, along_x)):
+            for other, target in partners:
+                signal_if(other < here, answers.at[axis], target)
+
+    for load in loads[4:]:
+        load.start()
+    pl.semaphore_wait(barrier, greetings)
+    answer()
 
     def remote(src, dst, send, recv, target):
         return pltpu.make_async_remote_copy(
@@ -156,7 +193,7 @@
     ]
     state_swap = remote(local_other, local_in, swap_send.at[4], swap_recv.at[4], sib)
 
-    for load in loads[4:7]:
+    for load in loads[2:4]:
         load.wait()
 
     starts = [jnp.int32(0)]
@@ -172,10 +209,6 @@
     flag0 = carries(y * (2 * ZN) + 2 * z)
     flag1 = carries(y * (2 * ZN) + 2 * z + 1)
     slope = [slopes[HALF * core + i] for i in range(HALF)]
-    for i in range(HALF):
-        begin = pl.multiple_of(core * WIDE + i * HD, HD)
-        gain[:, i * HD : (i + 1) * HD] = gain_flat[pl.ds(begin, HD)].reshape(1, HD)
-
     def cols(i):
         return pl.ds(pl.multiple_of(i * HD, HD), HD)
 
@@ -194,8 +227,9 @@
         local_other[i] = local_state(
             k_other[:, cols(i)], v_other[:, cols(i)], HALF * (1 - core) + i
         ).astype(BF16)
-    loads[2].wait()
-    loads[3].wait()
+    state_swap.start()
+    loads[4].wait()
+    loads[5].wait()
     for i in range(HALF):
         local[i] = local_state(k[own, cols(i)], v[own, cols(i)], HALF * core + i)
 
@@ -208,13 +242,6 @@
 
     def shares_of(i):
         return [next_door] if i is near else [PER * i + j for j in range(PER)]
-
-    share_slope = slopes[HALF * core + z // PER]
-    lam2 = jnp.exp(jnp.full((1, HD), -1.0 * PAIR, F32) * share_slope)
-    step_decay = [
-        lam2 * (carries(y * (2 * ZN) + 2 * j) * carries(y * (2 * ZN) + 2 * j + 1))
-        for j in range(ZN)
-    ]
 
     def share_copy(phase, other):
         return remote(
@@ -225,6 +252,15 @@
             at_z(other),
         )
 
+    def share_arrival(phase, other):
+        return remote(
+            share_out.at[phase, z],
+            share_in.at[phase, other],
+            share_send.at[phase, other],
+            share_recv.at[phase, other],
+            at_z(other),
+        )
+
     def back_copy(phase, other):
         return remote(
             back_out.at[phase, other],
@@ -234,8 +270,11 @@
             at_z(other),
         )
 
+    def put_shares(phase, i, value):
+        share_out[phase, pl.ds(PER * i, PER)] = value.astype(BF16).reshape(PER, SHARE, HD)
+
     def send_shares(phase, i, value):
-        share_out[phase, pl.ds(PER * i, PER)] = value.astype(BF16).reshape(PER, SHARE, HD)
+        put_shares(phase, i, value)
         for other in shares_of(i):
             share_copy(phase, other).start()
         if i is near:
@@ -243,13 +282,7 @@
 
     def turn(phase, backward):
         for other in ring[::-1]:
-            remote(
-                share_out.at[phase, z],
-                share_in.at[phase, other],
-                share_send.at[phase, other],
-                share_recv.at[phase, other],
-                at_z(other),
-            ).wait_recv()
+            share_arrival(phase, other).wait_recv()
         order = range(ZN - 1, -1, -1) if backward else range(ZN)
         total = jnp.zeros((SHARE, HD), F32)
         product = jnp.ones((1, HD), F32)
@@ -264,7 +297,7 @@
             carry_in.at[phase],
             carry_send.at[phase],
             carry_recv.at[phase],
-            down if backward else up,
+            below(z) if backward else above(z),
         )
         carry.start()
         carry.wait_recv()
@@ -292,14 +325,37 @@
     def state(phase, i):
         return back_in[phase, pl.ds(PER * i, PER)].reshape(HD, HD)
 
-    pl.semaphore_wait(barrier, len(partners))
-    state_swap.start()
     state_swap.wait_recv()
-    for i in send_order:
-        send_shares(0, i, local[i] + local_in[i].astype(F32))
+    for i in range(HALF):
+        put_shares(0, i, local[i] + local_in[i].astype(F32))
+    share_in[0, z] = share_out[0, z]
+    for other in ring:
+
+        @pl.when(other < z)
+        def _():
+            share_copy(0, other).start()
+
+    for other in range(1, ZN):
+
+        @pl.when(other > z)
+        def _():
+            pl.semaphore_wait(answers.at[other], 1)
+            share_copy(0, other).start()
+
     for swap in swaps:
         swap.start()
 
+    share_slope = slopes[HALF * core + z // PER]
+    lam2 = jnp.exp(jnp.full((1, HD), -1.0 * PAIR, F32) * share_slope)
+    step_decay = [
+        lam2 * (carries(y * (2 * ZN) + 2 * j) * carries(y * (2 * ZN) + 2 * j + 1))
+        for j in range(ZN)
+    ]
+
+    loads[6].wait()
+    for i in range(HALF):
+        begin = pl.multiple_of(core * WIDE + i * HD, HD)
+        gain[:, i * HD : (i + 1) * HD] = gain_flat[pl.ds(begin, HD)].reshape(1, HD)
     token = lax.broadcasted_iota(jnp.int32, (PAIR, HD), 0)
     second = token >= TOK
     token_f = token.astype(F32)
@@ -324,6 +380,7 @@
         weights[i] = weight
         raw[:, cols(i)] = dot(weight, v[:, cols(i)], 1, 0)
 
+    wait_some(answers.at[ZN], 2 - lower_y)
     turn(0, False)
     squares = jnp.zeros((PAIR, HD), F32)
     products = jnp.zeros((PAIR, HD), F32)
@@ -343,6 +400,7 @@
         jnp.where(place < 2, token_row(squares[:TOK]), token_row(squares[TOK:])),
         jnp.where(place < 6, token_row(products[:TOK]), token_row(products[TOK:])),
     )
+    wait_some(answers.at[ZN + 1], 2 * (XN - 1 - x))
     sum_copies = []
     for index, target in cross:
         copy = remote(
@@ -496,6 +554,7 @@
             shares,
             shares,
             pltpu.VMEM((2 * XN, 8, HD), F32),
+            pltpu.SemaphoreType.REGULAR((ZN + 2,)),
             dma((9,)),
             dma((2,)),
             dma((5,)),

time: 50.6 us -> 49.6 us (0.980); the launches traced: 50.4 us -> 48.9 us
  Pallas kernels: 49.8 us -> 48.2 us
    pallas_call x1, Pallas kernels: 48.8 us -> 47.2 us  [body(): pl.pallas_call(functools.partial(kernel, features), out_shape=(pltpu.VMEM...]
where the time goes in v4:
time: 49.6 us; the launch traced here: 48.9 us
  Pallas kernels  48.2 us (97%)
  between operations  0.64 us (1%)
    pallas_call x1, Pallas kernels, body(): pl.pallas_call(functools.partial(kernel, features), out_shape=(pltpu.VMEM...  47.2 us
    pallas_call x1, Pallas kernels, body(): pl.pallas_call(place_results, out_shape=(whole,) * 4, in_specs=[in_vmem]...  1 us

profile of v4, /device:TPU:1, one launch (start us, length us, event | category | flops | bytes accessed | tf_op | source)
XLA Modules:
  0.0 48.9 jit_solution(16548896171564444485)
XLA Ops:
  0.6 47.2 %lightning.1 = (bf16[128,1024]{1,0:T(8,128)(2,1)S(1)}, bf16[128,1024]{1,0:T(8,128)(2,1)S(1)}, bf16[128,1024]{1,0:T(8,128)(2,1)S(1)}, bf16[128,1024]{1,0:T(8,128)(2,1)S(1)}) custom-call(f32[8]{0:T(128)} %slopes_hbm.1, s32[16]{0:T(128)} %doc_hbm.1, bf16[128,1024]{1,0:T(8,128)(2,1)} %q_hbm.1, bf16[128,1024]{1,0:T(8,128)(2,1)} %k_hbm.1, ...), custom_call_target="tpu_custom_call" | custom-call | tf_op jit(solution)/shard_map/lightning/pallas_call | solution.py:521
  47.9 1.0 %place.1 = (bf16[128,1024]{1,0:T(8,128)(2,1)}, bf16[128,1024]{1,0:T(8,128)(2,1)}, bf16[128,1024]{1,0:T(8,128)(2,1)}, bf16[128,1024]{1,0:T(8,128)(2,1)}) custom-call(bf16[128,1024]{1,0:T(8,128)(2,1)S(1)} %get-tuple-element.8.refs_0_, bf16[128,1024]{1,0:T(8,128)(2,1)S(1)} %get-tuple-element.9.refs_1_, bf16[128,1024]{1,0:T(8,128)(2,1)S(1)} %get-tuple-element.10.refs_2_, ...), custom_call_target="tpu_custom_call" | custom-call | tf_op jit(solution)/shard_map/place/pallas_call | solution.py:585

commit v5 on v4

--- a/solution.py
+++ b/solution.py
@@ -68,6 +68,8 @@
     carry_in,
     back_out,
     back_in,
+    kept,
+    to_end_decay,
     sums,
     answers,
     local_sem,
@@ -281,16 +283,10 @@
             share_in[phase, z] = share_out[phase, z]
 
     def turn(phase, backward):
+        total = share_in[phase, z].astype(F32) * to_end_decay[phase, z]
         for other in ring[::-1]:
             share_arrival(phase, other).wait_recv()
-        order = range(ZN - 1, -1, -1) if backward else range(ZN)
-        total = jnp.zeros((SHARE, HD), F32)
-        product = jnp.ones((1, HD), F32)
-        before, products = {}, {}
-        for j in order:
-            before[j], products[j] = total, product
-            total = total * step_decay[j] + share_in[phase, j].astype(F32)
-            product = product * step_decay[j]
+            total = total + share_in[phase, other].astype(F32) * to_end_decay[phase, other]
         carry_out[phase] = total.astype(BF16)
         carry = remote(
             carry_out.at[phase],
@@ -300,13 +296,29 @@
             below(z) if backward else above(z),
         )
         carry.start()
+        inside = jnp.zeros((SHARE, HD), F32)
+        for j in range(ZN - 1, -1, -1) if backward else range(ZN):
+            kept[j] = inside
+            inside = inside * step_decay[j] + share_in[phase, j].astype(F32)
         carry.wait_recv()
         incoming = carry_in[phase].astype(F32)
-        for j in range(ZN):
-            back_out[phase, j] = (before[j] + products[j] * incoming).astype(BF16)
-        for other in ring:
-            back_copy(phase, other).start()
-        back_in[phase, z] = back_out[phase, z]
+        if backward:
+            for other in range(ZN):
+                back_out[phase, other] = (
+                    kept[other] + to_end_decay[2 + phase, other] * incoming
+                ).astype(BF16)
+
+                @pl.when(other != z)
+                def _():
+                    back_copy(phase, other).start()
+
+        else:
+            for other in ring:
+                back_out[phase, other] = (
+                    kept[other] + to_end_decay[2 + phase, other] * incoming
+                ).astype(BF16)
+                back_copy(phase, other).start()
+        back_in[phase, z] = (kept[z] + to_end_decay[2 + phase, z] * incoming).astype(BF16)
         for other in ring:
             share_copy(phase, other).wait_send()
         carry.wait_send()
@@ -351,6 +363,15 @@
         lam2 * (carries(y * (2 * ZN) + 2 * j) * carries(y * (2 * ZN) + 2 * j + 1))
         for j in range(ZN)
     ]
+
+    after, ahead = jnp.ones((1, HD), F32), jnp.ones((1, HD), F32)
+    for j in range(ZN):
+        to_end_decay[1, j] = after
+        to_end_decay[2, j] = after
+        to_end_decay[0, ZN - 1 - j] = ahead
+        to_end_decay[3, ZN - 1 - j] = ahead
+        after = after * step_decay[j]
+        ahead = ahead * step_decay[ZN - 1 - j]
 
     loads[6].wait()
     for i in range(HALF):
@@ -553,6 +574,8 @@
             carry,
             shares,
             shares,
+            pltpu.VMEM((ZN, SHARE, HD), F32),
+            pltpu.VMEM((4, ZN, 1, HD), F32),
             pltpu.VMEM((2 * XN, 8, HD), F32),
             pltpu.SemaphoreType.REGULAR((ZN + 2,)),
             dma((9,)),

time: 49.6 us -> 49.1 us (0.990)
  no operation moved by 1% of the time
where the time goes in v5:
time: 49.1 us; the launch traced here: 48.6 us
  Pallas kernels  47.9 us (98%)
  between operations  0.64 us (1%)
    pallas_call x1, Pallas kernels, body(): pl.pallas_call(functools.partial(kernel, features), out_shape=(pltpu.VMEM...  46.9 us
    pallas_call x1, Pallas kernels, body(): pl.pallas_call(place_results, out_shape=(whole,) * 4, in_specs=[in_vmem]...  1 us

profile of v5, /device:TPU:1, one launch (start us, length us, event | category | flops | bytes accessed | tf_op | source)
XLA Modules:
  0.0 48.6 jit_solution(7493290428879154939)
XLA Ops:
  0.6 46.9 %lightning.1 = (bf16[128,1024]{1,0:T(8,128)(2,1)S(1)}, bf16[128,1024]{1,0:T(8,128)(2,1)S(1)}, bf16[128,1024]{1,0:T(8,128)(2,1)S(1)}, bf16[128,1024]{1,0:T(8,128)(2,1)S(1)}) custom-call(f32[8]{0:T(128)} %slopes_hbm.1, s32[16]{0:T(128)} %doc_hbm.1, bf16[128,1024]{1,0:T(8,128)(2,1)} %q_hbm.1, bf16[128,1024]{1,0:T(8,128)(2,1)} %k_hbm.1, ...), custom_call_target="tpu_custom_call" | custom-call | tf_op jit(solution)/shard_map/lightning/pallas_call | solution.py:542
  47.6 1.0 %place.1 = (bf16[128,1024]{1,0:T(8,128)(2,1)}, bf16[128,1024]{1,0:T(8,128)(2,1)}, bf16[128,1024]{1,0:T(8,128)(2,1)}, bf16[128,1024]{1,0:T(8,128)(2,1)}) custom-call(bf16[128,1024]{1,0:T(8,128)(2,1)S(1)} %get-tuple-element.8.refs_0_, bf16[128,1024]{1,0:T(8,128)(2,1)S(1)} %get-tuple-element.9.refs_1_, bf16[128,1024]{1,0:T(8,128)(2,1)S(1)} %get-tuple-element.10.refs_2_, ...), custom_call_target="tpu_custom_call" | custom-call | tf_op jit(solution)/shard_map/place/pallas_call | solution.py:608

commit v6 on v5

--- a/solution.py
+++ b/solution.py
@@ -70,8 +70,11 @@
     back_in,
     kept,
     to_end_decay,
+    early_in,
     sums,
     answers,
+    early_send,
+    early_recv,
     local_sem,
     own_sem,
     swap_send,
@@ -157,8 +160,10 @@
     for here, partners in ((z, along_z), (y, along_y), (x, along_x)):
         for other, target in partners:
             signal_if(other > here, barrier, target)
+    for other, _ in along_z:
+        signal_if((z == 0) & (other > 0), barrier, above(other))
     lower_y = (next_y < y).astype(jnp.int32) + (last_y < y).astype(jnp.int32)
-    greetings = 1 + z + lower_y + 2 * x
+    greetings = 1 + z + lower_y + 2 * x + (z > 0).astype(jnp.int32)
 
     def wait_some(semaphore, count):
         @pl.when(count > 0)
@@ -281,6 +286,30 @@
             share_copy(phase, other).start()
         if i is near:
             share_in[phase, z] = share_out[phase, z]
+
+    def early_copy():
+        return remote(
+            carry_out.at[1], early_in.at[z], early_send.at[0], early_recv.at[z], below(0)
+        )
+
+    def add_early(i):
+        @pl.when(z == 0)
+        def _():
+            decay = jnp.exp(
+                jnp.full((1, HD), -1.0 * PAIR * (ZN - 1), F32) * slopes[HALF * core + i]
+            )
+            decay = decay * row_flag
+            for share in shares_of(i):
+                remote(
+                    carry_out.at[1],
+                    early_in.at[share],
+                    early_send.at[0],
+                    early_recv.at[share],
+                    sib,
+                ).wait_recv()
+                back_in[1, share] = (
+                    back_in[1, share].astype(F32) + decay * early_in[share].astype(F32)
+                ).astype(BF16)
 
     def turn(phase, backward):
         total = share_in[phase, z].astype(F32) * to_end_decay[phase, z]
@@ -300,10 +329,18 @@
         for j in range(ZN - 1, -1, -1) if backward else range(ZN):
             kept[j] = inside
             inside = inside * step_decay[j] + share_in[phase, j].astype(F32)
+        if backward:
+            back_out[1, 0] = kept[0].astype(BF16)
+
+            @pl.when(z != 0)
+            def _():
+                early_copy().start()
+                back_copy(1, 0).start()
+
         carry.wait_recv()
         incoming = carry_in[phase].astype(F32)
         if backward:
-            for other in range(ZN):
+            for other in range(1, ZN):
                 back_out[phase, other] = (
                     kept[other] + to_end_decay[2 + phase, other] * incoming
                 ).astype(BF16)
@@ -322,6 +359,11 @@
         for other in ring:
             share_copy(phase, other).wait_send()
         carry.wait_send()
+        if backward:
+
+            @pl.when(z != 0)
+            def _():
+                early_copy().wait_send()
 
     def arrived(phase, i):
         for other in shares_of(i):
@@ -359,10 +401,13 @@
 
     share_slope = slopes[HALF * core + z // PER]
     lam2 = jnp.exp(jnp.full((1, HD), -1.0 * PAIR, F32) * share_slope)
-    step_decay = [
-        lam2 * (carries(y * (2 * ZN) + 2 * j) * carries(y * (2 * ZN) + 2 * j + 1))
-        for j in range(ZN)
+    row_flags = [
+        carries(y * (2 * ZN) + 2 * j) * carries(y * (2 * ZN) + 2 * j + 1) for j in range(ZN)
     ]
+    step_decay = [lam2 * flag for flag in row_flags]
+    row_flag = row_flags[1]
+    for j in range(2, ZN):
+        row_flag = row_flag * row_flags[j]
 
     after, ahead = jnp.ones((1, HD), F32), jnp.ones((1, HD), F32)
     for j in range(ZN):
@@ -492,7 +537,9 @@
 
     finals = []
     for i in use_order:
-        grad_state = arrived(1, i)
+        arrived(1, i)
+        add_early(i)
+        grad_state = state(1, i)
         for j, (part, operand, side, target) in enumerate(
             ((dk_part, v, 1, dk_out), (dv_part, k, 0, dv_out))
         ):
@@ -576,8 +623,11 @@
             shares,
             pltpu.VMEM((ZN, SHARE, HD), F32),
             pltpu.VMEM((4, ZN, 1, HD), F32),
+            pltpu.VMEM((ZN, SHARE, HD), BF16),
             pltpu.VMEM((2 * XN, 8, HD), F32),
             pltpu.SemaphoreType.REGULAR((ZN + 2,)),
+            dma((1,)),
+            dma((ZN,)),
             dma((9,)),
             dma((2,)),
             dma((5,)),

time: 49.1 us -> 48.9 us (level)
  no operation moved by 1% of the time
where the time goes in v6:
time: 48.9 us; the launch traced here: 48.8 us
  Pallas kernels  48.1 us (98%)
  between operations  0.64 us (1%)
    pallas_call x1, Pallas kernels, body(): pl.pallas_call(functools.partial(kernel, features), out_shape=(pltpu.VMEM...  47.1 us
    pallas_call x1, Pallas kernels, body(): pl.pallas_call(place_results, out_shape=(whole,) * 4, in_specs=[in_vmem]...  1 us

profile of v6, /device:TPU:1, one launch (start us, length us, event | category | flops | bytes accessed | tf_op | source)
XLA Modules:
  0.0 48.8 jit_solution(13210305097399191993)
XLA Ops:
  0.6 47.1 %lightning.1 = (bf16[128,1024]{1,0:T(8,128)(2,1)S(1)}, bf16[128,1024]{1,0:T(8,128)(2,1)S(1)}, bf16[128,1024]{1,0:T(8,128)(2,1)S(1)}, bf16[128,1024]{1,0:T(8,128)(2,1)S(1)}) custom-call(f32[8]{0:T(128)} %slopes_hbm.1, s32[16]{0:T(128)} %doc_hbm.1, bf16[128,1024]{1,0:T(8,128)(2,1)} %q_hbm.1, bf16[128,1024]{1,0:T(8,128)(2,1)} %k_hbm.1, ...), custom_call_target="tpu_custom_call" | custom-call | tf_op jit(solution)/shard_map/lightning/pallas_call | solution.py:589
  47.8 1.0 %place.1 = (bf16[128,1024]{1,0:T(8,128)(2,1)}, bf16[128,1024]{1,0:T(8,128)(2,1)}, bf16[128,1024]{1,0:T(8,128)(2,1)}, bf16[128,1024]{1,0:T(8,128)(2,1)}) custom-call(bf16[128,1024]{1,0:T(8,128)(2,1)S(1)} %get-tuple-element.8.refs_0_, bf16[128,1024]{1,0:T(8,128)(2,1)S(1)} %get-tuple-element.9.refs_1_, bf16[128,1024]{1,0:T(8,128)(2,1)S(1)} %get-tuple-element.10.refs_2_, ...), custom_call_target="tpu_custom_call" | custom-call | tf_op jit(solution)/shard_map/place/pallas_call | solution.py:658

commit v7 on v6

--- a/solution.py
+++ b/solution.py
@@ -324,6 +324,12 @@
             carry_recv.at[phase],
             below(z) if backward else above(z),
         )
+        if backward:
+
+            @pl.when(z != 0)
+            def _():
+                early_copy().start()
+
         carry.start()
         inside = jnp.zeros((SHARE, HD), F32)
         for j in range(ZN - 1, -1, -1) if backward else range(ZN):
@@ -334,7 +340,6 @@
 
             @pl.when(z != 0)
             def _():
-                early_copy().start()
                 back_copy(1, 0).start()
 
         carry.wait_recv()

time: 48.9 us -> 48.8 us (level)
  no operation moved by 1% of the time
where the time goes in v7:
time: 48.8 us; the launch traced here: 48.7 us
  Pallas kernels  48 us (98%)
  between operations  0.64 us (1%)
    pallas_call x1, Pallas kernels, body(): pl.pallas_call(functools.partial(kernel, features), out_shape=(pltpu.VMEM...  47 us
    pallas_call x1, Pallas kernels, body(): pl.pallas_call(place_results, out_shape=(whole,) * 4, in_specs=[in_vmem]...  1 us

profile of v7, /device:TPU:1, one launch (start us, length us, event | category | flops | bytes accessed | tf_op | source)
XLA Modules:
  0.0 48.7 jit_solution(6788256182973227910)
XLA Ops:
  0.6 47.0 %lightning.1 = (bf16[128,1024]{1,0:T(8,128)(2,1)S(1)}, bf16[128,1024]{1,0:T(8,128)(2,1)S(1)}, bf16[128,1024]{1,0:T(8,128)(2,1)S(1)}, bf16[128,1024]{1,0:T(8,128)(2,1)S(1)}) custom-call(f32[8]{0:T(128)} %slopes_hbm.1, s32[16]{0:T(128)} %doc_hbm.1, bf16[128,1024]{1,0:T(8,128)(2,1)} %q_hbm.1, bf16[128,1024]{1,0:T(8,128)(2,1)} %k_hbm.1, ...), custom_call_target="tpu_custom_call" | custom-call | tf_op jit(solution)/shard_map/lightning/pallas_call | solution.py:594
  47.7 1.0 %place.1 = (bf16[128,1024]{1,0:T(8,128)(2,1)}, bf16[128,1024]{1,0:T(8,128)(2,1)}, bf16[128,1024]{1,0:T(8,128)(2,1)}, bf16[128,1024]{1,0:T(8,128)(2,1)}) custom-call(bf16[128,1024]{1,0:T(8,128)(2,1)S(1)} %get-tuple-element.8.refs_0_, bf16[128,1024]{1,0:T(8,128)(2,1)S(1)} %get-tuple-element.9.refs_1_, bf16[128,1024]{1,0:T(8,128)(2,1)S(1)} %get-tuple-element.10.refs_2_, ...), custom_call_target="tpu_custom_call" | custom-call | tf_op jit(solution)/shard_map/place/pallas_call | solution.py:663
